TPU v7x, 128 devices: a whole 4x4x4 slice. The times are simulated.
128 devices in a mesh: gx: 8 (over z, x_hi), gy: 8 (over y, core), gz: 2 (over x_lo).
Axes of the slice: x: 4 (x_hi: 2, x_lo: 2; x = x_hi * 2 + x_lo), y: 4, z: 4, core: 2. Of those that a mesh axis runs over, the one named last changes fastest.
Arguments:
- field: float32 [4, 2048, 2048], P('gz', 'gx', 'gy'), may hold values from -6 to 6
- start_x: float32 [2048, 256], P('gx'), may hold values from -6 to 6
- start_y: float32 [2048, 256], P('gy'), may hold values from -6 to 6
Outputs:
- basis_x: float32 [2048, 256], P('gx')
- basis_y: float32 [2048, 256], P('gy')
- core: float32 [4, 256, 256], P('gz', 'gx', 'gy')
All inputs are finite; a program needn't handle non-finite values.
Results may differ from a plain program's by a relative error of at most 0.0003.
Values sent between devices are 32-bit elements; how exact they have to be, the bound alone decides.
A program may use at most 128 MiB of HBM per device.

v0:
```python
import jax
import jax.numpy as jnp
from jax import lax
from jax.sharding import PartitionSpec as P

ITERS = 4


def orthonormal_local(product_image, cross_gram):
    factor = jnp.linalg.cholesky(cross_gram)
    return lax.linalg.triangular_solve(
        factor, product_image, left_side=False, lower=True, transpose_a=True
    )


def contract_outer(left_block, right_block):
    return lax.dot_general(
        left_block, right_block, (((0, 2), (0, 2)), ((), ())), precision=lax.Precision.HIGHEST
    )


def local(field, start_x, start_y):
    partial_gram = contract_outer(field, lax.all_gather(field, "gx", axis=1, tiled=True))
    gram_x = lax.psum(partial_gram, ("gy", "gz"))
    basis_x = start_x
    for iteration in range(ITERS):
        product_image = jnp.dot(
            gram_x,
            lax.all_gather(basis_x, "gx", axis=0, tiled=True),
            precision=lax.Precision.HIGHEST,
        )
        local_cross = jnp.dot(product_image.T, product_image, precision=lax.Precision.HIGHEST)
        cross_gram = lax.psum(local_cross, "gx")
        basis_x = orthonormal_local(product_image, cross_gram)
    rank_slice = basis_x
    projected = lax.psum_scatter(
        jnp.einsum("xa,sxy->asy", rank_slice, field, precision=lax.Precision.HIGHEST),
        "gx",
        scatter_dimension=0,
        tiled=True,
    )
    partial_gram_y = lax.dot_general(
        projected,
        lax.all_gather(projected, "gy", axis=2, tiled=True),
        (((0, 1), (0, 1)), ((), ())),
        precision=lax.Precision.HIGHEST,
    )
    gram_y = lax.psum(partial_gram_y, ("gx", "gz"))
    basis_y = start_y
    for iteration in range(ITERS):
        product_image = jnp.dot(
            gram_y,
            lax.all_gather(basis_y, "gy", axis=0, tiled=True),
            precision=lax.Precision.HIGHEST,
        )
        local_cross = jnp.dot(product_image.T, product_image, precision=lax.Precision.HIGHEST)
        cross_gram = lax.psum(local_cross, "gy")
        basis_y = orthonormal_local(product_image, cross_gram)
    rank_slice = basis_y
    core_turned = lax.psum_scatter(
        jnp.einsum("yc,asy->cas", rank_slice, projected, precision=lax.Precision.HIGHEST),
        "gy",
        scatter_dimension=0,
        tiled=True,
    )
    core = jnp.transpose(core_turned, (2, 1, 0))
    return (basis_x, basis_y, core)


def solution(mesh):
    return jax.shard_map(
        local,
        mesh=mesh,
        in_specs=(P("gz", "gx", "gy"), P("gx", None), P("gy", None)),
        out_specs=(P("gx", None), P("gy", None), P("gz", "gx", "gy")),
        check_vma=False,
    )
```

profile of v0, /device:TPU:0, one launch (start us, length us, event | category | flops | bytes accessed | tf_op | source)
XLA Modules:
  0.0 1845.0 jit_solution(16931272757001872655)
XLA Ops:
  9.5 75.7 %all-gather.10.cloned.1.call-done = f32[2,2048,256]{2,1,0:T(8,128)} async-done(((f32[2,256,256]{2,1,0:T(8,128)}), f32[2,2048,256]{2,1,0:T(8,128)}) %all-gather.10.cloned.1.call-update) | async-done | bytes 4194320 | tf_op jit(solution)/shard_map/all_gather | solution.py:23
  92.6 46.9 %all-gather.12.cloned.1.call-done = f32[2048,256]{1,0:T(8,128)} async-done(((f32[256,256]{1,0:T(8,128)}), f32[2048,256]{1,0:T(8,128)}) %all-gather.12.cloned.1.call-update) | async-done | bytes 2097168 | tf_op jit(solution)/shard_map/all_gather | solution.py:29
  139.5 135.0 %all-reduce.12.cloned.1.call-done = f32[256,2048]{1,0:T(8,128)} async-done(((f32[256,2048]{1,0:T(8,128)}), f32[256,2048]{1,0:T(8,128)}) %all-reduce.12.cloned.1.call-update) | async-done | bytes 2097168 | tf_op jit(solution)/shard_map/psum | solution.py:24
  280.2 84.4 %all-reduce.14.cloned.1.call-done = f32[256,256]{0,1:T(8,128)} async-done(((f32[256,256]{0,1:T(8,128)}), f32[256,256]{0,1:T(8,128)}) %all-reduce.14.cloned.1.call-update) | async-done | bytes 262160 | tf_op jit(solution)/shard_map/psum | solution.py:33
  407.0 19.7 %custom-call.26 = f32[2,128,128]{1,2,0:T(8,128)S(1)} custom-call(f32[2,128,128]{2,1,0:T(8,128)S(1)} %get-tuple-element.55), custom_call_target="InvertDiagBlocksLowerTriangular" | custom-call | tf_op jit(solution)/shard_map/triangular_solve/custom-call.0 | solution.py:11
  428.5 52.3 %all-gather.14.cloned.1.call-done = f32[2048,256]{0,1:T(8,128)} async-done(((f32[256,256]{0,1:T(8,128)}), f32[2048,256]{0,1:T(8,128)}) %all-gather.14.cloned.1.call-update) | async-done | bytes 2097168 | tf_op jit(solution)/shard_map/all_gather | solution.py:29
  485.6 82.6 %all-reduce.16.cloned.1.call-done = f32[256,256]{0,1:T(8,128)} async-done(((f32[256,256]{0,1:T(8,128)}), f32[256,256]{0,1:T(8,128)}) %all-reduce.16.cloned.1.call-update) | async-done | bytes 262160 | tf_op jit(solution)/shard_map/psum | solution.py:33
  611.1 19.7 %custom-call.28 = f32[2,128,128]{1,2,0:T(8,128)S(1)} custom-call(f32[2,128,128]{2,1,0:T(8,128)S(1)} %get-tuple-element.56), custom_call_target="InvertDiagBlocksLowerTriangular" | custom-call | tf_op jit(solution)/shard_map/triangular_solve/custom-call.0 | solution.py:11
  632.7 52.3 %all-gather.16.cloned.1.call-done = f32[2048,256]{0,1:T(8,128)} async-done(((f32[256,256]{0,1:T(8,128)}), f32[2048,256]{0,1:T(8,128)}) %all-gather.16.cloned.1.call-update) | async-done | bytes 2097168 | tf_op jit(solution)/shard_map/all_gather | solution.py:29
  689.8 82.5 %all-reduce.18.cloned.1.call-done = f32[256,256]{0,1:T(8,128)} async-done(((f32[256,256]{0,1:T(8,128)}), f32[256,256]{0,1:T(8,128)}) %all-reduce.18.cloned.1.call-update) | async-done | bytes 262160 | tf_op jit(solution)/shard_map/psum | solution.py:33
  815.5 19.7 %custom-call.30 = f32[2,128,128]{1,2,0:T(8,128)S(1)} custom-call(f32[2,128,128]{2,1,0:T(8,128)S(1)} %get-tuple-element.57), custom_call_target="InvertDiagBlocksLowerTriangular" | custom-call | tf_op jit(solution)/shard_map/triangular_solve/custom-call.0 | solution.py:11
  837.0 52.3 %all-gather.18.cloned.1.call-done = f32[2048,256]{0,1:T(8,128)} async-done(((f32[256,256]{0,1:T(8,128)}), f32[2048,256]{0,1:T(8,128)}) %all-gather.18.cloned.1.call-update) | async-done | bytes 2097168 | tf_op jit(solution)/shard_map/all_gather | solution.py:29
  894.1 82.5 %all-reduce.20.cloned.1.call-done = f32[256,256]{0,1:T(8,128)} async-done(((f32[256,256]{0,1:T(8,128)}), f32[256,256]{0,1:T(8,128)}) %all-reduce.20.cloned.1.call-update) | async-done | bytes 262160 | tf_op jit(solution)/shard_map/psum | solution.py:33
  1042.4 67.6 %reduce-scatter.3.cloned.1.call-done = f32[32,2,256]{2,0,1:T(8,128)} async-done(((f32[256,2,256]{2,0,1:T(8,128)}), f32[32,2,256]{2,0,1:T(8,128)}) %reduce-scatter.3.cloned.1.call-update) | async-done | bytes 65552 | tf_op jit(solution)/shard_map/reduce_scatter | solution.py:36
  1127.8 88.8 %all-reduce.22.cloned.1.call-done = f32[256,2048]{1,0:T(8,128)} async-done(((f32[256,2048]{1,0:T(8,128)}), f32[256,2048]{1,0:T(8,128)}) %all-reduce.22.cloned.1.call-update) | async-done | bytes 2097168 | tf_op jit(solution)/shard_map/psum | solution.py:48
  1222.3 58.8 %all-reduce.24.cloned.1.call-done = f32[256,256]{0,1:T(8,128)} async-done(((f32[256,256]{0,1:T(8,128)}), f32[256,256]{0,1:T(8,128)}) %all-reduce.24.cloned.1.call-update) | async-done | bytes 262160 | tf_op jit(solution)/shard_map/psum | solution.py:57
  1345.5 24.3 %all-gather.22.cloned.1.call-done = f32[2048,256]{0,1:T(8,128)} async-done(((f32[256,256]{0,1:T(8,128)}), f32[2048,256]{0,1:T(8,128)}) %all-gather.22.cloned.1.call-update) | async-done | bytes 2097168 | tf_op jit(solution)/shard_map/all_gather | solution.py:53
  1374.6 59.9 %all-reduce.26.cloned.1.call-done = f32[256,256]{0,1:T(8,128)} async-done(((f32[256,256]{0,1:T(8,128)}), f32[256,256]{0,1:T(8,128)}) %all-reduce.26.cloned.1.call-update) | async-done | bytes 262160 | tf_op jit(solution)/shard_map/psum | solution.py:57
  1477.5 19.7 %custom-call.36 = f32[2,128,128]{1,2,0:T(8,128)S(1)} custom-call(f32[2,128,128]{2,1,0:T(8,128)S(1)} %get-tuple-element.60), custom_call_target="InvertDiagBlocksLowerTriangular" | custom-call | tf_op jit(solution)/shard_map/triangular_solve/custom-call.0 | solution.py:11
  1499.0 24.3 %all-gather.24.cloned.1.call-done = f32[2048,256]{0,1:T(8,128)} async-done(((f32[256,256]{0,1:T(8,128)}), f32[2048,256]{0,1:T(8,128)}) %all-gather.24.cloned.1.call-update) | async-done | bytes 2097168 | tf_op jit(solution)/shard_map/all_gather | solution.py:53
  1528.1 59.9 %all-reduce.28.cloned.1.call-done = f32[256,256]{0,1:T(8,128)} async-done(((f32[256,256]{0,1:T(8,128)}), f32[256,256]{0,1:T(8,128)}) %all-reduce.28.cloned.1.call-update) | async-done | bytes 262160 | tf_op jit(solution)/shard_map/psum | solution.py:57
  1652.5 24.3 %all-gather.26.cloned.1.call-done = f32[2048,256]{0,1:T(8,128)} async-done(((f32[256,256]{0,1:T(8,128)}), f32[2048,256]{0,1:T(8,128)}) %all-gather.26.cloned.1.call-update) | async-done | bytes 2097168 | tf_op jit(solution)/shard_map/all_gather | solution.py:53
  1681.6 59.9 %all-reduce.30.cloned.1.call-done = f32[256,256]{0,1:T(8,128)} async-done(((f32[256,256]{0,1:T(8,128)}), f32[256,256]{0,1:T(8,128)}) %all-reduce.30.cloned.1.call-update) | async-done | bytes 262160 | tf_op jit(solution)/shard_map/psum | solution.py:57
  1807.8 27.7 %reduce-scatter.5.cloned.1.call-done = f32[32,32,2]{1,0,2:T(8,128)} async-done(((f32[256,32,2]{1,0,2:T(8,128)}), f32[32,32,2]{1,0,2:T(8,128)}) %reduce-scatter.5.cloned.1.call-update) | async-done | bytes 8208 | tf_op jit(solution)/shard_map/reduce_scatter | solution.py:60
  (288 shorter events, 528.8 us)
Async XLA Ops:
  8.0 77.2 %all-gather.10.cloned.1.call-start = ((), (), s32[]{:S(2)}) async-start(), calls=%async_computation.2 | async-start | bytes 4718592 | tf_op jit(solution)/shard_map/all_gather | solution.py:23
  8.7 130.8 %all-gather.12.cloned.1.call-start = ((), (), s32[]{:S(2)}) async-start(), calls=%async_computation.4 | async-start | bytes 2359296 | tf_op jit(solution)/shard_map/all_gather | solution.py:29
  9.5 265.0 %all-reduce.12.cloned.1.call-start = ((), (), s32[]{:S(2)}) async-start(), calls=%async_computation.3 | async-start | bytes 4194304 | tf_op jit(solution)/shard_map/psum | solution.py:24
  92.6 272.0 %all-reduce.14.cloned.1.call-start = ((), (), s32[]{:S(2)}) async-start(), calls=%async_computation.5 | async-start | bytes 524288 | tf_op jit(solution)/shard_map/psum | solution.py:33
  279.9 200.9 %all-gather.14.cloned.1.call-start = ((), (), s32[]{:S(2)}) async-start(), calls=%async_computation.6 | async-start | bytes 2359296 | tf_op jit(solution)/shard_map/all_gather | solution.py:29
  388.3 92.5 %copy-start = (f32[256,2048]{1,0:T(8,128)S(1)}, f32[256,2048]{1,0:T(8,128)}, u32[]{:S(2)}) copy-start(f32[256,2048]{1,0:T(8,128)} %all-reduce.12.cloned.1.call-done) | copy-start | bytes 6291460
  428.5 139.7 %all-reduce.16.cloned.1.call-start = ((), (), s32[]{:S(2)}) async-start(), calls=%async_computation.7 | async-start | bytes 524288 | tf_op jit(solution)/shard_map/psum | solution.py:33
  485.6 199.4 %all-gather.16.cloned.1.call-start = ((), (), s32[]{:S(2)}) async-start(), calls=%async_computation.8 | async-start | bytes 2359296 | tf_op jit(solution)/shard_map/all_gather | solution.py:29
  632.6 139.7 %all-reduce.18.cloned.1.call-start = ((), (), s32[]{:S(2)}) async-start(), calls=%async_computation.9 | async-start | bytes 524288 | tf_op jit(solution)/shard_map/psum | solution.py:33
  689.7 199.6 %all-gather.18.cloned.1.call-start = ((), (), s32[]{:S(2)}) async-start(), calls=%async_computation.10 | async-start | bytes 2359296 | tf_op jit(solution)/shard_map/all_gather | solution.py:29
  837.0 139.7 %all-reduce.20.cloned.1.call-start = ((), (), s32[]{:S(2)}) async-start(), calls=%async_computation.11 | async-start | bytes 524288 | tf_op jit(solution)/shard_map/psum | solution.py:33
  894.1 215.9 %reduce-scatter.3.cloned.1.call-start = ((), (), s32[]{:S(2)}) async-start(), calls=%async_computation.12 | async-start | bytes 589824 | tf_op jit(solution)/shard_map/reduce_scatter | solution.py:36
  978.8 61.6 %copy-start.2 = (f32[2,256,256]{2,1,0:T(8,128)S(1)}, f32[2,256,256]{2,1,0:T(8,128)}, u32[]{:S(2)}) copy-start(f32[2,256,256]{2,1,0:T(8,128)} %param.6) | copy-start | bytes 1572868
  1041.8 86.0 %all-gather.20.cloned.1.call-start = ((), (), s32[]{:S(2)}) async-start(), calls=%async_computation.14 | async-start | bytes 2359296 | tf_op jit(solution)/shard_map/all_gather | solution.py:53
  1042.4 174.2 %all-reduce.22.cloned.1.call-start = ((), (), s32[]{:S(2)}) async-start(), calls=%async_computation.13 | async-start | bytes 4194304 | tf_op jit(solution)/shard_map/psum | solution.py:48
  1127.7 153.4 %all-reduce.24.cloned.1.call-start = ((), (), s32[]{:S(2)}) async-start(), calls=%async_computation.15 | async-start | bytes 524288 | tf_op jit(solution)/shard_map/psum | solution.py:57
  1222.0 147.8 %all-gather.22.cloned.1.call-start = ((), (), s32[]{:S(2)}) async-start(), calls=%async_computation.16 | async-start | bytes 2359296 | tf_op jit(solution)/shard_map/all_gather | solution.py:53
  1294.9 74.9 %copy-start.1 = (f32[256,2048]{1,0:T(8,128)S(1)}, f32[256,2048]{1,0:T(8,128)}, u32[]{:S(2)}) copy-start(f32[256,2048]{1,0:T(8,128)} %all-reduce.22.cloned.1.call-done) | copy-start | bytes 6291460
  1345.5 89.0 %all-reduce.26.cloned.1.call-start = ((), (), s32[]{:S(2)}) async-start(), calls=%async_computation.17 | async-start | bytes 524288 | tf_op jit(solution)/shard_map/psum | solution.py:57
  1374.6 148.7 %all-gather.24.cloned.1.call-start = ((), (), s32[]{:S(2)}) async-start(), calls=%async_computation.18 | async-start | bytes 2359296 | tf_op jit(solution)/shard_map/all_gather | solution.py:53
  1498.9 89.0 %all-reduce.28.cloned.1.call-start = ((), (), s32[]{:S(2)}) async-start(), calls=%async_computation.19 | async-start | bytes 524288 | tf_op jit(solution)/shard_map/psum | solution.py:57
  1528.0 148.7 %all-gather.26.cloned.1.call-start = ((), (), s32[]{:S(2)}) async-start(), calls=%async_computation.20 | async-start | bytes 2359296 | tf_op jit(solution)/shard_map/all_gather | solution.py:53
  1652.4 89.0 %all-reduce.30.cloned.1.call-start = ((), (), s32[]{:S(2)}) async-start(), calls=%async_computation.21 | async-start | bytes 524288 | tf_op jit(solution)/shard_map/psum | solution.py:57
  1681.5 154.0 %reduce-scatter.5.cloned.1.call-start = ((), (), s32[]{:S(2)}) async-start(), calls=%async_computation.22 | async-start | bytes 294912 | tf_op jit(solution)/shard_map/reduce_scatter | solution.py:60
  (1 other events, 61.5 us)
Sparse Core Ops, SparseCore 0:
  11.1 74.0 all-gather.9
  87.6 51.9 all-gather.11
  142.0 132.4 all-reduce.11
  280.1 84.5 all-reduce.13
  428.6 52.1 all-gather.13
  485.7 82.4 all-reduce.15
  632.7 52.1 all-gather.15
  689.8 82.4 all-reduce.17
  837.1 52.1 all-gather.17
  894.2 82.4 all-reduce.19
  1041.9 68.0 reduce-scatter.2
  1127.8 88.6 all-reduce.21
Sparse Core Ops, SparseCore 1:
  1044.0 22.9 all-gather.19
  1222.1 58.9 all-reduce.23
  1345.5 24.2 all-gather.21
  1374.7 59.8 all-reduce.25
  1499.0 24.2 all-gather.23
  1528.1 59.8 all-reduce.27
  1652.5 24.2 all-gather.25
  1681.6 59.8 all-reduce.29
  1806.2 29.3 reduce-scatter.4
where the time goes:
time: 1850 us; the launch traced here: 1840 us
  waiting for transfers between devices  1240 us (67%)
  other arithmetic  446 us (24%)
  matrix products  65.1 us (4%)
  local copies, waits for them, and re-layouts  44.1 us (2%)
  between operations  27.8 us (2%)
    psum x4, waiting for transfers between devices, local(): cross_gram = lax.psum(local_cross, 'gx')  332 us
    another operation x55, other arithmetic, orthonormal_local(): factor = jnp.linalg.cholesky(cross_gram)  276 us
    psum x4, waiting for transfers between devices, local(): cross_gram = lax.psum(local_cross, 'gy')  238 us
    all_gather x4, waiting for transfers between devices, local(): lax.all_gather(basis_x, 'gx', axis=0, tiled=True)  204 us
    another operation x25, other arithmetic, orthonormal_local(): lax.linalg.triangular_solve(factor, product_image, left_side=False, lower...  162 us
    psum x1, waiting for transfers between devices, local(): gram_x = lax.psum(partial_gram, ('gy', 'gz'))  135 us
    psum x1, waiting for transfers between devices, local(): gram_y = lax.psum(partial_gram_y, ('gx', 'gz'))  88.8 us
    all_gather x1, waiting for transfers between devices, local(): lax.all_gather(field, 'gx', axis=1, tiled=True)  75.7 us
  transfers between devices with their start and end apart: 21, of which 20 were waited for; matrix products, arithmetic and copies ran while one was open for 1% of the time, Pallas kernels for 0%

commit v1 on v0

--- a/solution.py
+++ b/solution.py
@@ -1,15 +1,118 @@
 import jax
 import jax.numpy as jnp
 from jax import lax
+from jax.experimental import pallas as pl
+from jax.experimental.pallas import tpu as pltpu
 from jax.sharding import PartitionSpec as P
 
 ITERS = 4
 
+RANK = 256
+PANEL = 32
+LANES = 128
+SUB = 8
+
+
+def split3(v):
+    hi = v.astype(jnp.bfloat16)
+    rest = v - hi.astype(jnp.float32)
+    mid = rest.astype(jnp.bfloat16)
+    low = (rest - mid.astype(jnp.float32)).astype(jnp.bfloat16)
+    return hi, mid, low
+
+
+def eliminate_panel(work, base, panel):
+    tiles, width = PANEL // SUB, 2 * RANK // LANES
+    rows = work[pl.ds(base, PANEL), :]
+    turned = pltpu.roll(rows[:, :RANK], RANK - base, 1)
+    cols = [
+        [jnp.broadcast_to(turned[SUB * q:SUB * q + SUB, c:c + 1], (SUB, LANES)) for q in range(tiles)]
+        for c in range(PANEL)
+    ]
+    body = [[rows[SUB * q:SUB * q + SUB, LANES * t:LANES * t + LANES] for t in range(width)] for q in range(tiles)]
+    place = lax.broadcasted_iota(jnp.int32, (SUB, LANES), 0)
+    pivots = [jnp.ones((SUB, LANES), jnp.float32) for _ in range(tiles)]
+
+    def across(tile, s):
+        return jnp.broadcast_to(tile[s:s + 1, :], (SUB, LANES))
+
+    for c in range(PANEL):
+        first, s = c // SUB, c % SUB
+        column = cols[c]
+        pivot = across(column[first], s)
+        inverse = 1.0 / pivot
+        pivots[first] = jnp.where(place == s, pivot, pivots[first])
+        below = [None] * tiles
+        for q in range(first, tiles):
+            below[q] = jnp.where(place > s, column[q], 0.0) if q == first else column[q]
+        scaled = [None if b is None else b * inverse for b in below]
+        for later in range(c + 1, PANEL):
+            own = across(column[later // SUB], later % SUB)
+            for q in range(later // SUB, tiles):
+                if later == c + 1:
+                    cols[later][q] = cols[later][q] - (below[q] * own) * inverse
+                else:
+                    cols[later][q] = cols[later][q] - scaled[q] * own
+        for t in range(width):
+            row = across(body[first][t], s)
+            for q in range(first, tiles):
+                body[q][t] = body[q][t] - scaled[q] * row
+    scale = [lax.rsqrt(p) for p in pivots]
+    done = jnp.concatenate(
+        [jnp.concatenate([body[q][t] * scale[q] for t in range(width)], axis=1) for q in range(tiles)], axis=0
+    )
+    work[pl.ds(base, PANEL), :] = done
+    return done
+
+
+def cholesky_inverse(work, between=None):
+    def step(panel, carry):
+        base = pl.multiple_of(panel * PANEL, PANEL)
+        if between is not None:
+            between(panel)
+        done = eliminate_panel(work, base, panel)
+        lane = lax.broadcasted_iota(jnp.int32, (PANEL, RANK), 1)
+        left = jnp.where(lane >= base + PANEL, done[:, :RANK], 0.0)
+        lh, lm, ll = split3(left)
+        rh, rm, rl = split3(done)
+        lhs = jnp.concatenate([lh, lh, lm, lh, lm, ll], axis=0)
+        rhs = jnp.concatenate([rh, rm, rh, rl, rm, rh], axis=0)
+        work[...] -= lax.dot_general(lhs, rhs, (((0,), (0,)), ((), ())), preferred_element_type=jnp.float32)
+        return carry
+
+    lax.fori_loop(0, RANK // PANEL, step, 0)
+
+
+def eye_tail():
+    r = lax.broadcasted_iota(jnp.int32, (RANK, RANK), 0)
+    c = lax.broadcasted_iota(jnp.int32, (RANK, RANK), 1)
+    return jnp.where(r == c, 1.0, 0.0).astype(jnp.float32)
+
+
+def chol_kernel(c_ref, w_ref, work):
+    work[:, :RANK] = c_ref[...]
+    work[:, RANK:] = eye_tail()
+    cholesky_inverse(work)
+    w_ref[...] = work[:, RANK:]
+
+
+def inverse_factor(c):
+    return pl.pallas_call(
+        chol_kernel,
+        out_shape=jax.ShapeDtypeStruct((RANK, RANK), jnp.float32),
+        in_specs=[pl.BlockSpec(memory_space=pltpu.VMEM)],
+        out_specs=pl.BlockSpec(memory_space=pltpu.VMEM),
+        scratch_shapes=[pltpu.VMEM((RANK, 2 * RANK), jnp.float32)],
+        compiler_params=pltpu.CompilerParams(vmem_limit_bytes=32 * 2**20),
+    )(c)
+
 
 def orthonormal_local(product_image, cross_gram):
-    factor = jnp.linalg.cholesky(cross_gram)
-    return lax.linalg.triangular_solve(
-        factor, product_image, left_side=False, lower=True, transpose_a=True
+    return lax.dot_general(
+        product_image,
+        inverse_factor(cross_gram),
+        (((1,), (1,)), ((), ())),
+        precision=lax.Precision.HIGHEST,
     )
 
 

time: 1850 us -> 1420 us (0.77)
  other arithmetic: 446 us -> 0 us
  Pallas kernels: 0 us -> 65.1 us
  local copies, waits for them, and re-layouts: 44.1 us -> 9.07 us
    another operation x80 -> x0, other arithmetic: 438 us -> none  [the longest x55 276 us: orthonormal_local(): factor = jnp.linalg.cholesky(cross_gram)]
    pallas_call x0 -> x8, Pallas kernels: none -> 65.1 us  [inverse_factor(): pl.pallas_call(chol_kernel, out_shape=jax.ShapeDtypeStruct((RANK, RANK),...]
    another operation x73 -> x0, local copies, waits for them, and re-layouts: 32.4 us -> none  [the longest x57 32.2 us: orthonormal_local(): lax.linalg.triangular_solve(factor, product_image, left_side=False, lower...]
where the time goes in v1:
time: 1420 us; the launch traced here: 1410 us
  waiting for transfers between devices  1240 us (87%)
  Pallas kernels  65.1 us (5%)
  matrix products  61.4 us (4%)
  between operations  16.4 us (1%)
    psum x4, waiting for transfers between devices, local(): cross_gram = lax.psum(local_cross, 'gx')  332 us
    psum x4, waiting for transfers between devices, local(): cross_gram = lax.psum(local_cross, 'gy')  239 us
    all_gather x4, waiting for transfers between devices, local(): lax.all_gather(basis_x, 'gx', axis=0, tiled=True)  202 us
    psum x1, waiting for transfers between devices, local(): gram_x = lax.psum(partial_gram, ('gy', 'gz'))  135 us
    psum x1, waiting for transfers between devices, local(): gram_y = lax.psum(partial_gram_y, ('gx', 'gz'))  88.6 us
    all_gather x1, waiting for transfers between devices, local(): lax.all_gather(field, 'gx', axis=1, tiled=True)  75.7 us
    all_gather x4, waiting for transfers between devices, local(): lax.all_gather(basis_y, 'gy', axis=0, tiled=True)  72.6 us
    reduce_scatter x1, waiting for transfers between devices, local(): lax.psum_scatter(jnp.einsum('xa,sxy->asy', rank_slice, field, precision=l...  67.6 us
  transfers between devices with their start and end apart: 21, of which 20 were waited for; matrix products, arithmetic and copies ran while one was open for 1% of the time, Pallas kernels for 0%

profile of v1, /device:TPU:0, one launch (start us, length us, event | category | flops | bytes accessed | tf_op | source)
XLA Modules:
  0.0 1411.1 jit_solution(536736361504694)
XLA Ops:
  9.5 75.7 %all-gather.10.cloned.1.call-done = f32[2,2048,256]{2,1,0:T(8,128)} async-done(((f32[2,256,256]{2,1,0:T(8,128)}), f32[2,2048,256]{2,1,0:T(8,128)}) %all-gather.10.cloned.1.call-update) | async-done | bytes 4194320 | tf_op jit(solution)/shard_map/all_gather | solution.py:126
  92.7 46.8 %all-gather.12.cloned.1.call-done = f32[2048,256]{1,0:T(8,128)} async-done(((f32[256,256]{1,0:T(8,128)}), f32[2048,256]{1,0:T(8,128)}) %all-gather.12.cloned.1.call-update) | async-done | bytes 2097168 | tf_op jit(solution)/shard_map/all_gather | solution.py:132
  139.5 135.0 %all-reduce.11.cloned.1.call-done = f32[256,2048]{1,0:T(8,128)} async-done(((f32[256,2048]{1,0:T(8,128)}), f32[256,2048]{1,0:T(8,128)}) %all-reduce.11.cloned.1.call-update) | async-done | bytes 2097168 | tf_op jit(solution)/shard_map/psum | solution.py:127
  280.1 84.6 %all-reduce.13.cloned.1.call-done.c_ref = f32[256,256]{1,0:T(8,128)} async-done(((f32[256,256]{1,0:T(8,128)}), f32[256,256]{1,0:T(8,128)}) %all-reduce.13.cloned.1.call-update) | async-done | bytes 262160 | tf_op jit(solution)/shard_map/psum | solution.py:136
  375.0 51.9 %all-gather.14.cloned.1.call-done = f32[2048,256]{1,0:T(8,128)} async-done(((f32[256,256]{1,0:T(8,128)}), f32[2048,256]{1,0:T(8,128)}) %all-gather.14.cloned.1.call-update) | async-done | bytes 2097168 | tf_op jit(solution)/shard_map/all_gather | solution.py:132
  431.7 82.5 %all-reduce.15.cloned.1.call-done.c_ref = f32[256,256]{1,0:T(8,128)} async-done(((f32[256,256]{1,0:T(8,128)}), f32[256,256]{1,0:T(8,128)}) %all-reduce.15.cloned.1.call-update) | async-done | bytes 262160 | tf_op jit(solution)/shard_map/psum | solution.py:136
  515.2 8.1 shard_map.59
  525.0 51.4 %all-gather.16.cloned.1.call-done = f32[2048,256]{1,0:T(8,128)} async-done(((f32[256,256]{1,0:T(8,128)}), f32[2048,256]{1,0:T(8,128)}) %all-gather.16.cloned.1.call-update) | async-done | bytes 2097168 | tf_op jit(solution)/shard_map/all_gather | solution.py:132
  581.2 82.5 %all-reduce.17.cloned.1.call-done.c_ref = f32[256,256]{1,0:T(8,128)} async-done(((f32[256,256]{1,0:T(8,128)}), f32[256,256]{1,0:T(8,128)}) %all-reduce.17.cloned.1.call-update) | async-done | bytes 262160 | tf_op jit(solution)/shard_map/psum | solution.py:136
  664.7 8.1 shard_map.60
  674.0 51.8 %all-gather.18.cloned.1.call-done = f32[2048,256]{1,0:T(8,128)} async-done(((f32[256,256]{1,0:T(8,128)}), f32[2048,256]{1,0:T(8,128)}) %all-gather.18.cloned.1.call-update) | async-done | bytes 2097168 | tf_op jit(solution)/shard_map/all_gather | solution.py:132
  730.7 82.5 %all-reduce.19.cloned.1.call-done.c_ref = f32[256,256]{1,0:T(8,128)} async-done(((f32[256,256]{1,0:T(8,128)}), f32[256,256]{1,0:T(8,128)}) %all-reduce.19.cloned.1.call-update) | async-done | bytes 262160 | tf_op jit(solution)/shard_map/psum | solution.py:136
  814.2 8.2 shard_map.61
  824.8 67.6 %reduce-scatter.3.cloned.1.call-done = f32[32,2,256]{2,0,1:T(8,128)} async-done(((f32[256,2,256]{2,0,1:T(8,128)}), f32[32,2,256]{2,0,1:T(8,128)}) %reduce-scatter.3.cloned.1.call-update) | async-done | bytes 65552 | tf_op jit(solution)/shard_map/reduce_scatter | solution.py:139
  892.4 13.7 all_gather.35
  910.4 88.6 %all-reduce.21.cloned.1.call-done = f32[256,2048]{1,0:T(8,128)} async-done(((f32[256,2048]{1,0:T(8,128)}), f32[256,2048]{1,0:T(8,128)}) %all-reduce.21.cloned.1.call-update) | async-done | bytes 2097168 | tf_op jit(solution)/shard_map/psum | solution.py:151
  1004.7 59.0 %all-reduce.23.cloned.1.call-done.c_ref = f32[256,256]{1,0:T(8,128)} async-done(((f32[256,256]{1,0:T(8,128)}), f32[256,256]{1,0:T(8,128)}) %all-reduce.23.cloned.1.call-update) | async-done | bytes 262160 | tf_op jit(solution)/shard_map/psum | solution.py:160
  1074.0 24.3 %all-gather.22.cloned.1.call-done = f32[2048,256]{1,0:T(8,128)} async-done(((f32[256,256]{1,0:T(8,128)}), f32[2048,256]{1,0:T(8,128)}) %all-gather.22.cloned.1.call-update) | async-done | bytes 2097168 | tf_op jit(solution)/shard_map/all_gather | solution.py:156
  1103.1 59.9 %all-reduce.25.cloned.1.call-done.c_ref = f32[256,256]{1,0:T(8,128)} async-done(((f32[256,256]{1,0:T(8,128)}), f32[256,256]{1,0:T(8,128)}) %all-reduce.25.cloned.1.call-update) | async-done | bytes 262160 | tf_op jit(solution)/shard_map/psum | solution.py:160
  1173.3 24.3 %all-gather.24.cloned.1.call-done = f32[2048,256]{1,0:T(8,128)} async-done(((f32[256,256]{1,0:T(8,128)}), f32[2048,256]{1,0:T(8,128)}) %all-gather.24.cloned.1.call-update) | async-done | bytes 2097168 | tf_op jit(solution)/shard_map/all_gather | solution.py:156
  1202.4 59.9 %all-reduce.27.cloned.1.call-done.c_ref = f32[256,256]{1,0:T(8,128)} async-done(((f32[256,256]{1,0:T(8,128)}), f32[256,256]{1,0:T(8,128)}) %all-reduce.27.cloned.1.call-update) | async-done | bytes 262160 | tf_op jit(solution)/shard_map/psum | solution.py:160
  1272.7 24.1 %all-gather.26.cloned.1.call-done = f32[2048,256]{1,0:T(8,128)} async-done(((f32[256,256]{1,0:T(8,128)}), f32[2048,256]{1,0:T(8,128)}) %all-gather.26.cloned.1.call-update) | async-done | bytes 2097168 | tf_op jit(solution)/shard_map/all_gather | solution.py:156
  1301.6 59.9 %all-reduce.29.cloned.1.call-done.c_ref = f32[256,256]{1,0:T(8,128)} async-done(((f32[256,256]{1,0:T(8,128)}), f32[256,256]{1,0:T(8,128)}) %all-reduce.29.cloned.1.call-update) | async-done | bytes 262160 | tf_op jit(solution)/shard_map/psum | solution.py:160
  1372.4 29.4 %reduce-scatter.5.cloned.1.call-done = f32[32,32,2]{1,0,2:T(8,128)} async-done(((f32[256,32,2]{1,0,2:T(8,128)}), f32[32,32,2]{1,0,2:T(8,128)}) %reduce-scatter.5.cloned.1.call-update) | async-done | bytes 8208 | tf_op jit(solution)/shard_map/reduce_scatter | solution.py:163
  (105 shorter events, 115.1 us)
Async XLA Ops:
  8.0 77.2 %all-gather.10.cloned.1.call-start = ((), (), s32[]{:S(2)}) async-start(), calls=%async_computation.2 | async-start | bytes 4718592 | tf_op jit(solution)/shard_map/all_gather | solution.py:126
  8.7 130.8 %all-gather.12.cloned.1.call-start = ((), (), s32[]{:S(2)}) async-start(), calls=%async_computation.4 | async-start | bytes 2359296 | tf_op jit(solution)/shard_map/all_gather | solution.py:132
  9.5 265.0 %all-reduce.11.cloned.1.call-start = ((), (), s32[]{:S(2)}) async-start(), calls=%async_computation.3 | async-start | bytes 4194304 | tf_op jit(solution)/shard_map/psum | solution.py:127
  92.6 272.1 %all-reduce.13.cloned.1.call-start = ((), (), s32[]{:S(2)}) async-start(), calls=%async_computation.5 | async-start | bytes 524288 | tf_op jit(solution)/shard_map/psum | solution.py:136
  274.5 152.4 %copy-start.8 = (f32[256,2048]{1,0:T(8,128)S(1)}, f32[256,2048]{1,0:T(8,128)}, u32[]{:S(2)}) copy-start(f32[256,2048]{1,0:T(8,128)} %all-reduce.11.cloned.1.call-done) | copy-start | bytes 6291460
  280.1 146.8 %all-gather.14.cloned.1.call-start = ((), (), s32[]{:S(2)}) async-start(), calls=%async_computation.6 | async-start | bytes 2359296 | tf_op jit(solution)/shard_map/all_gather | solution.py:132
  375.0 139.2 %all-reduce.15.cloned.1.call-start = ((), (), s32[]{:S(2)}) async-start(), calls=%async_computation.7 | async-start | bytes 524288 | tf_op jit(solution)/shard_map/psum | solution.py:136
  431.7 144.7 %all-gather.16.cloned.1.call-start = ((), (), s32[]{:S(2)}) async-start(), calls=%async_computation.8 | async-start | bytes 2359296 | tf_op jit(solution)/shard_map/all_gather | solution.py:132
  524.5 139.3 %all-reduce.17.cloned.1.call-start = ((), (), s32[]{:S(2)}) async-start(), calls=%async_computation.9 | async-start | bytes 524288 | tf_op jit(solution)/shard_map/psum | solution.py:136
  581.2 144.7 %all-gather.18.cloned.1.call-start = ((), (), s32[]{:S(2)}) async-start(), calls=%async_computation.10 | async-start | bytes 2359296 | tf_op jit(solution)/shard_map/all_gather | solution.py:132
  674.0 139.2 %all-reduce.19.cloned.1.call-start = ((), (), s32[]{:S(2)}) async-start(), calls=%async_computation.11 | async-start | bytes 524288 | tf_op jit(solution)/shard_map/psum | solution.py:136
  729.4 93.4 %copy-start.10 = (f32[2,256,256]{2,1,0:T(8,128)S(1)}, f32[2,256,256]{2,1,0:T(8,128)}, u32[]{:S(2)}) copy-start(f32[2,256,256]{2,1,0:T(8,128)} %param.3) | copy-start | bytes 1572868
  730.7 161.7 %reduce-scatter.3.cloned.1.call-start = ((), (), s32[]{:S(2)}) async-start(), calls=%async_computation.12 | async-start | bytes 589824 | tf_op jit(solution)/shard_map/reduce_scatter | solution.py:139
  824.2 86.2 %all-gather.20.cloned.1.call-start = ((), (), s32[]{:S(2)}) async-start(), calls=%async_computation.14 | async-start | bytes 2359296 | tf_op jit(solution)/shard_map/all_gather | solution.py:156
  824.8 174.2 %all-reduce.21.cloned.1.call-start = ((), (), s32[]{:S(2)}) async-start(), calls=%async_computation.13 | async-start | bytes 4194304 | tf_op jit(solution)/shard_map/psum | solution.py:151
  910.2 153.5 %all-reduce.23.cloned.1.call-start = ((), (), s32[]{:S(2)}) async-start(), calls=%async_computation.15 | async-start | bytes 524288 | tf_op jit(solution)/shard_map/psum | solution.py:160
  999.0 99.2 %copy-start.9 = (f32[256,2048]{1,0:T(8,128)S(1)}, f32[256,2048]{1,0:T(8,128)}, u32[]{:S(2)}) copy-start(f32[256,2048]{1,0:T(8,128)} %all-reduce.21.cloned.1.call-done) | copy-start | bytes 6291460
  1004.6 93.6 %all-gather.22.cloned.1.call-start = ((), (), s32[]{:S(2)}) async-start(), calls=%async_computation.16 | async-start | bytes 2359296 | tf_op jit(solution)/shard_map/all_gather | solution.py:156
  1073.9 89.0 %all-reduce.25.cloned.1.call-start = ((), (), s32[]{:S(2)}) async-start(), calls=%async_computation.17 | async-start | bytes 524288 | tf_op jit(solution)/shard_map/psum | solution.py:160
  1103.0 94.5 %all-gather.24.cloned.1.call-start = ((), (), s32[]{:S(2)}) async-start(), calls=%async_computation.18 | async-start | bytes 2359296 | tf_op jit(solution)/shard_map/all_gather | solution.py:156
  1173.2 89.0 %all-reduce.27.cloned.1.call-start = ((), (), s32[]{:S(2)}) async-start(), calls=%async_computation.19 | async-start | bytes 524288 | tf_op jit(solution)/shard_map/psum | solution.py:160
  1202.3 94.5 %all-gather.26.cloned.1.call-start = ((), (), s32[]{:S(2)}) async-start(), calls=%async_computation.20 | async-start | bytes 2359296 | tf_op jit(solution)/shard_map/all_gather | solution.py:156
  1272.5 89.0 %all-reduce.29.cloned.1.call-start = ((), (), s32[]{:S(2)}) async-start(), calls=%async_computation.21 | async-start | bytes 524288 | tf_op jit(solution)/shard_map/psum | solution.py:160
  1301.6 100.2 %reduce-scatter.5.cloned.1.call-start = ((), (), s32[]{:S(2)}) async-start(), calls=%async_computation.22 | async-start | bytes 294912 | tf_op jit(solution)/shard_map/reduce_scatter | solution.py:163
  (11 other events, 197.9 us)
Sparse Core Ops, SparseCore 0:
  11.1 74.0 all-gather.9
  87.6 51.9 all-gather.11
  142.0 132.4 all-reduce.10
  280.2 84.5 all-reduce.12
  375.1 51.7 all-gather.13
  431.8 82.3 all-reduce.14
  524.6 51.7 all-gather.15
  581.3 82.3 all-reduce.16
  674.1 51.7 all-gather.17
  730.8 82.3 all-reduce.18
  824.3 68.0 reduce-scatter.2
  910.3 88.7 all-reduce.20
Sparse Core Ops, SparseCore 1:
  826.4 22.9 all-gather.19
  1004.7 58.9 all-reduce.22
  1074.0 24.2 all-gather.21
  1103.1 59.8 all-reduce.24
  1173.3 24.2 all-gather.23
  1202.4 59.8 all-reduce.26
  1272.5 24.2 all-gather.25
  1301.7 59.8 all-reduce.28
  1372.5 29.3 reduce-scatter.4
